TPU v7x, 128 devices: a whole 4x4x4 slice. The times are simulated.
128 devices in a mesh: vid: 16 (over z, y), aud: 8 (over x, core).
Axes of the slice: x: 4, y: 4, z: 4, core: 2. Of those that a mesh axis runs over, the one named last changes fastest.
Arguments:
- video_q: bfloat16 [65536, 2048], P('vid', 'aud'), may hold values from -6 to 6
- video_k: bfloat16 [65536, 2048], P('vid', 'aud'), may hold values from -6 to 6
- video_v: bfloat16 [65536, 2048], P('vid', 'aud'), may hold values from -6 to 6
- video_dout: bfloat16 [65536, 2048], P('vid', 'aud'), may hold values from -6 to 6
- audio_q: bfloat16 [16384, 2048], P(('vid', 'aud')), may hold values from -6 to 6
- audio_k: bfloat16 [16384, 2048], P(('vid', 'aud')), may hold values from -6 to 6
- audio_v: bfloat16 [16384, 2048], P(('vid', 'aud')), may hold values from -6 to 6
- audio_dout: bfloat16 [16384, 2048], P(('vid', 'aud')), may hold values from -6 to 6
- video_pairs: int32 [128, 8], replicated, may hold values from 0 to 127, as said below
- audio_pairs: int32 [128, 8], replicated, may hold values from 0 to 127, as said below
- video_len: int32 [128], replicated, may hold values from 64 to 512
- audio_len: int32 [128], replicated, may hold values from 16 to 128
Outputs:
- video_out: bfloat16 [65536, 2048], P('vid', 'aud')
- audio_out: bfloat16 [16384, 2048], P(('vid', 'aud'))
- video_dq: bfloat16 [65536, 2048], P('vid', 'aud')
- video_dk: bfloat16 [65536, 2048], P('vid', 'aud')
- video_dv: bfloat16 [65536, 2048], P('vid', 'aud')
- audio_dq: bfloat16 [16384, 2048], P(('vid', 'aud'))
- audio_dk: bfloat16 [16384, 2048], P(('vid', 'aud'))
- audio_dv: bfloat16 [16384, 2048], P(('vid', 'aud'))
Inputs may be any that keep to these rules, and one draw needn't show every extreme that they name: `video_pairs`: row b lists 8 consecutive audio blocks in increasing order, block b among them. `audio_pairs`: row b lists 8 consecutive video blocks in increasing order, block b among them.
All inputs are finite; a program needn't handle non-finite values.
Results may differ from a plain program's by a relative error of at most 0.024.
Values may be sent and summed in bfloat16 or wider, within the bound.
No kernel may reach another device: no remote copies, remote signals or barrier semaphores. Data moves between devices by JAX's collectives and lax.ppermute only.
A program may use at most 256 MiB of HBM per device.

v0:
```python
import math

import jax
import jax.numpy as jnp
from jax import lax
from jax.sharding import PartitionSpec as P

DH = 128
BV = 512
BA = 128
P_SIZE = 8


NEG_FILL = -1e30


def with_halo(array, sides, width):
    for axis, dim in sides:
        size, length = (lax.axis_size(axis), array.shape[dim])
        up = [(i, (i + 1) % size) for i in range(size - 1)]
        down = [(j, i) for i, j in up]
        last = lax.slice_in_dim(array, length - width, length, axis=dim)
        leading = lax.slice_in_dim(array, 0, width, axis=dim)
        before = lax.ppermute(last, axis, up)
        after = lax.ppermute(leading, axis, down)
        array = jnp.concatenate([before, array, after], axis=dim)
    return array


def shifted(block, axis, distance):
    devices = range(lax.axis_size(axis))
    route = [(i - distance, i) for i in devices if i - distance in devices]
    return lax.ppermute(block, axis, route)


def attend_tile(queries, keys, values, grad_out, key_valid):
    inv_root = 1.0 / math.sqrt(queries.shape[-1])
    scores = (
        jnp.einsum("rge,kge->grk", queries, keys, preferred_element_type=jnp.float32) * inv_root
    )
    scores = jnp.where(key_valid, scores, NEG_FILL)
    row_top = jnp.max(scores, axis=2, keepdims=True)
    exponent = jnp.where(key_valid, jnp.exp(scores - row_top), 0.0)
    row_total = jnp.sum(exponent, axis=2, keepdims=True)
    weights = exponent / row_total
    weights_half = weights.astype(jnp.bfloat16)
    outputs = jnp.einsum("grk,kge->rge", weights_half, values, preferred_element_type=jnp.float32)
    dprob = jnp.einsum("rge,kge->grk", grad_out, values, preferred_element_type=jnp.float32)
    delta_sum = jnp.sum(weights * dprob, axis=2, keepdims=True)
    dscore = (weights * (dprob - delta_sum)).astype(jnp.bfloat16)
    query_grad = (
        jnp.einsum("grk,kge->rge", dscore, keys, preferred_element_type=jnp.float32) * inv_root
    )
    key_grad = (
        jnp.einsum("grk,rge->kge", dscore, queries, preferred_element_type=jnp.float32) * inv_root
    )
    value_grad = jnp.einsum(
        "grk,rge->kge", weights_half, grad_out, preferred_element_type=jnp.float32
    )
    log_total = row_top[:, :, 0] + jnp.log(row_total[:, :, 0])
    return (outputs, query_grad, key_grad, value_grad, log_total, delta_sum[:, :, 0])


def add_rows(full, piece, start, axis):
    current = lax.dynamic_slice_in_dim(full, start, piece.shape[axis], axis)
    return lax.dynamic_update_slice_in_dim(full, current + piece, start, axis)


def fold_edges(accum, reach, rows, from_above, from_below):
    middle = accum[reach : reach + rows]
    lower_part = jnp.pad(from_below, ((0, rows - reach), (0, 0)))
    upper_part = jnp.pad(from_above, ((rows - reach, 0), (0, 0)))
    return (middle + lower_part + upper_part).astype(jnp.bfloat16)


def one_direction(queries, grad_out, near_pair, pairs, key_len, first_block, block_q, block_k):
    count = queries.shape[0] // block_q
    feature_width = queries.shape[1]
    heads_count = feature_width // DH
    offsets = jnp.arange(block_k, dtype=jnp.int32)
    empty = jnp.zeros((near_pair.shape[1], feature_width), jnp.float32)

    def step(carry, index):
        key_acc, value_acc = carry
        listed = lax.dynamic_index_in_dim(pairs, first_block + index, 0, keepdims=False)
        start = (listed[0] - first_block + P_SIZE - 1) * block_k
        key_tile = lax.dynamic_slice_in_dim(near_pair[0], start, P_SIZE * block_k, 0).reshape(
            P_SIZE * block_k, heads_count, DH
        )
        value_tile = lax.dynamic_slice_in_dim(near_pair[1], start, P_SIZE * block_k, 0).reshape(
            P_SIZE * block_k, heads_count, DH
        )
        lengths = lax.dynamic_slice_in_dim(key_len, listed[0], P_SIZE, 0)
        key_valid = (offsets[None, :] < lengths[:, None]).reshape(1, 1, -1)
        row_start = index * block_q
        query_tile = lax.dynamic_slice_in_dim(queries, row_start, block_q, 0).reshape(
            block_q, heads_count, DH
        )
        grad_tile = lax.dynamic_slice_in_dim(grad_out, row_start, block_q, 0).reshape(
            block_q, heads_count, DH
        )
        outputs, query_grad, key_grad, value_grad, log_total, delta_sum = attend_tile(
            query_tile, key_tile, value_tile, grad_tile, key_valid
        )
        key_acc = add_rows(key_acc, key_grad.reshape(-1, feature_width), start, 0)
        value_acc = add_rows(value_acc, value_grad.reshape(-1, feature_width), start, 0)
        return (
            (key_acc, value_acc),
            (
                outputs.reshape(block_q, feature_width).astype(jnp.bfloat16),
                query_grad.reshape(block_q, feature_width).astype(jnp.bfloat16),
                log_total,
                delta_sum,
            ),
        )

    (key_acc, value_acc), (outputs, query_grad, log_total, delta_sum) = lax.scan(
        step, (empty, empty), jnp.arange(count, dtype=jnp.int32)
    )
    return (
        outputs.reshape(-1, feature_width),
        query_grad.reshape(-1, feature_width),
        key_acc,
        value_acc,
        log_total,
        delta_sum,
    )


def per_device(
    video_q,
    video_k,
    video_v,
    video_dout,
    audio_q,
    audio_k,
    audio_v,
    audio_dout,
    video_pairs,
    audio_pairs,
    video_len,
    audio_len,
):
    vid_index = lax.axis_index("vid")
    blocks_here = video_q.shape[0] // BV
    first_block = vid_index * blocks_here
    audio_reach = (P_SIZE - 1) * BA
    video_reach = (P_SIZE - 1) * BV
    audio_rows = blocks_here * BA
    video_rows = blocks_here * BV
    audio_query, audio_key, audio_value, audio_grad = (
        lax.all_to_all(audio_q, "aud", split_axis=1, concat_axis=0, tiled=True),
        lax.all_to_all(audio_k, "aud", split_axis=1, concat_axis=0, tiled=True),
        lax.all_to_all(audio_v, "aud", split_axis=1, concat_axis=0, tiled=True),
        lax.all_to_all(audio_dout, "aud", split_axis=1, concat_axis=0, tiled=True),
    )
    audio_pair_near = with_halo(jnp.stack((audio_key, audio_value)), (("vid", 1),), audio_reach)
    video_out, video_dq, audio_key_acc, audio_value_acc, unused_log, unused_delta = one_direction(
        video_q, video_dout, audio_pair_near, video_pairs, audio_len, first_block, BV, BA
    )
    video_pair_near = with_halo(jnp.stack((video_k, video_v)), (("vid", 1),), video_reach)
    audio_out, audio_dq, video_key_acc, video_value_acc, log_rows, delta_rows = one_direction(
        audio_query, audio_grad, video_pair_near, audio_pairs, video_len, first_block, BA, BV
    )
    audio_lower = jnp.stack((audio_key_acc[:audio_reach], audio_value_acc[:audio_reach]))
    audio_upper = jnp.stack(
        (audio_key_acc[audio_reach + audio_rows :], audio_value_acc[audio_reach + audio_rows :])
    )
    video_lower = jnp.stack((video_key_acc[:video_reach], video_value_acc[:video_reach]))
    video_upper = jnp.stack(
        (video_key_acc[video_reach + video_rows :], video_value_acc[video_reach + video_rows :])
    )
    from_above = shifted(
        jnp.concatenate((audio_lower, video_lower), axis=1).astype(jnp.bfloat16), "vid", -1
    ).astype(jnp.float32)
    from_below = shifted(
        jnp.concatenate((audio_upper, video_upper), axis=1).astype(jnp.bfloat16), "vid", 1
    ).astype(jnp.float32)
    audio_above = from_above[:, :audio_reach]
    audio_below = from_below[:, :audio_reach]
    video_dk = fold_edges(
        video_key_acc,
        video_reach,
        video_rows,
        from_above[0, audio_reach:],
        from_below[0, audio_reach:],
    )
    video_dv = fold_edges(
        video_value_acc,
        video_reach,
        video_rows,
        from_above[1, audio_reach:],
        from_below[1, audio_reach:],
    )
    audio_key_sum = fold_edges(
        audio_key_acc, audio_reach, audio_rows, audio_above[0], audio_below[0]
    )
    audio_value_sum = fold_edges(
        audio_value_acc, audio_reach, audio_rows, audio_above[1], audio_below[1]
    )
    audio_out_back, audio_dq_back, audio_dk_back, audio_dv_back = (
        lax.all_to_all(audio_out, "aud", split_axis=0, concat_axis=1, tiled=True),
        lax.all_to_all(audio_dq, "aud", split_axis=0, concat_axis=1, tiled=True),
        lax.all_to_all(audio_key_sum, "aud", split_axis=0, concat_axis=1, tiled=True),
        lax.all_to_all(audio_value_sum, "aud", split_axis=0, concat_axis=1, tiled=True),
    )
    return (
        video_out,
        audio_out_back,
        video_dq,
        video_dk,
        video_dv,
        audio_dq_back,
        audio_dk_back,
        audio_dv_back,
    )


def solution(mesh):
    return jax.shard_map(
        per_device,
        mesh=mesh,
        in_specs=(
            P("vid", "aud"),
            P("vid", "aud"),
            P("vid", "aud"),
            P("vid", "aud"),
            P(("vid", "aud"), None),
            P(("vid", "aud"), None),
            P(("vid", "aud"), None),
            P(("vid", "aud"), None),
            P(),
            P(),
            P(),
            P(),
        ),
        out_specs=(
            P("vid", "aud"),
            P(("vid", "aud"), None),
            P("vid", "aud"),
            P("vid", "aud"),
            P("vid", "aud"),
            P(("vid", "aud"), None),
            P(("vid", "aud"), None),
            P(("vid", "aud"), None),
        ),
        check_vma=False,
    )
```

profile of v0, /device:TPU:24, one launch (start us, length us, event | category | flops | bytes accessed | tf_op | source)
XLA Modules:
  0.0 1277.2 jit_solution(948038151111390785)
XLA Ops:
  9.1 8.3 all-to-all-done
  21.9 9.3 all-to-all-done.1
  80.5 269.7 %while.42 = (s32[]{:T(128)}, f32[2816,256]{1,0:T(8,128)}, f32[2816,256]{1,0:T(8,128)}, bf16[8,512,256]{2,1,0:T(8,128)(2,1)}, bf16[8,512,256]{2,1,0:T(8,128)(2,1)...) while((s32[]{:T(128)}, f32[2816,256]{1,0:T(8,128)}, ...), condition=%wide.region_4.5_spmd.clone, body=%wide.region_0.4_spmd.clone.sunk | while | flops 1628570624 | bytes 97549496 | solution.py:117
  355.0 10.5 pad_maximum_fusion
  374.8 737.1 %while.43 = (s32[]{:T(128)}, f32[11264,256]{1,0:T(8,128)}, f32[11264,256]{1,0:T(8,128)}, bf16[8,128,256]{1,2,0:T(8,128)(2,1)S(1)}, bf16[8,128,256]{1,2,0:T(8,128...) while((s32[]{:T(128)}, f32[11264,256]{1,0:T(8,128)}, ...), condition=%wide.region_9.10_spmd.clone, body=%wide.region_5.9_spmd.clone.sunk | while | flops 1630641920 | bytes 202530960 | solution.py:117
  377.6 9.2 fusion.122
  415.6 5.7 copy.210
  421.3 6.2 bitcast_add_fusion.11
  427.5 5.6 copy.211
  442.5 5.7 copy.205
  448.2 6.1 bitcast_add_fusion.10
  459.9 7.4 constant_dynamic-update-slice_fusion.14
  469.8 9.2 fusion.122
  507.8 5.7 copy.210
  513.5 6.2 bitcast_add_fusion.11
  519.7 5.6 copy.211
  534.8 5.7 copy.205
  540.4 6.1 bitcast_add_fusion.10
  552.1 7.3 constant_dynamic-update-slice_fusion.14
  561.9 9.2 fusion.122
  599.9 5.7 copy.210
  605.7 6.2 bitcast_add_fusion.11
  626.9 5.7 copy.205
  632.5 6.1 bitcast_add_fusion.10
  644.2 7.3 constant_dynamic-update-slice_fusion.14
  654.0 9.2 fusion.122
  692.0 5.7 copy.210
  697.8 6.2 bitcast_add_fusion.11
  719.0 5.7 copy.205
  724.6 6.1 bitcast_add_fusion.10
  736.3 7.3 constant_dynamic-update-slice_fusion.14
  746.1 9.2 fusion.122
  784.2 5.7 copy.210
  789.9 6.2 bitcast_add_fusion.11
  796.0 5.6 copy.211
  811.1 5.7 copy.205
  816.7 6.1 bitcast_add_fusion.10
  828.4 7.3 constant_dynamic-update-slice_fusion.14
  838.2 9.2 fusion.122
  876.3 5.7 copy.210
  882.0 6.2 bitcast_add_fusion.11
  888.2 5.6 copy.211
  903.2 5.7 copy.205
  908.9 6.1 bitcast_add_fusion.10
  920.5 7.3 constant_dynamic-update-slice_fusion.14
  930.3 9.2 fusion.122
  968.4 5.7 copy.210
  974.1 6.2 bitcast_add_fusion.11
  995.3 5.7 copy.205
  1000.9 6.1 bitcast_add_fusion.10
  1012.6 7.2 constant_dynamic-update-slice_fusion.14
  1022.4 9.2 fusion.122
  1060.4 5.7 copy.210
  1066.1 6.2 bitcast_add_fusion.11
  1087.3 5.7 copy.205
  1093.0 6.1 bitcast_add_fusion.10
  1104.7 7.2 constant_dynamic-update-slice_fusion.14
  1111.9 5.8 convert.38
  1123.7 6.3 collective-permute-start.4
  1134.2 15.0 %all_to_all.140 = bf16[8,128,256]{1,2,0:T(8,128)(2,1)S(1)} all-to-all(bf16[8,128,256]{1,2,0:T(8,128)(2,1)S(1)} %get-tuple-element.525), channel_id=1, replica_groups=mesh['vid'=16,'aud'=8] {'aud'}, dimensions={0} | all-to-all | bytes 1048576 | tf_op jit(solution)/shard_map/all_to_all | solution.py:202
  1153.7 9.3 all-to-all-done.5
  1163.9 64.7 %collective-permute-done.4 = bf16[2,4480,256]{2,1,0:T(8,128)(2,1)} collective-permute-done((bf16[2,4480,256]{2,1,0:T(8,128)(2,1)}, bf16[2,4480,256]{2,1,0:T(8,128)(2,1)}, u32[]{:S(2)}, u32[]{:S(2)}) %collective-permute-start.4) | collective-permute-done | bytes 4587552 | tf_op jit(solution)/shard_map/ppermute | solution.py:33
  1250.5 6.6 slice_bitcast_fusion
  1264.3 10.3 add_convert_fusion
  (638 shorter events, 724.5 us)
Async XLA Ops:
  0.6 20.3 %copy-start.16 = (bf16[128,2048]{1,0:T(8,128)(2,1)S(1)}, bf16[128,2048]{1,0:T(8,128)(2,1)}, u32[]{:S(2)}) copy-start(bf16[128,2048]{1,0:T(8,128)(2,1)} %param.23) | copy-start | bytes 1572868
  2.7 14.6 %all-to-all-start = ((bf16[128,8,256]{0,2,1:T(8,128)(2,1)}), bf16[128,8,256]{0,2,1:T(8,128)(2,1)S(1)}, u32[]{:S(2)}, u32[]{:S(2)}) async-start(bf16[128,8,256]{0,2,1:T(8,128)(2,1)} %bitcast), calls=%async_computation | async-start | bytes 1048576 | tf_op jit(solution)/shard_map/all_to_all | solution.py:153
  17.4 13.8 %all-to-all-start.1 = ((bf16[128,8,256]{0,2,1:T(8,128)(2,1)}), bf16[128,8,256]{0,2,1:T(8,128)(2,1)S(1)}, u32[]{:S(2)}, u32[]{:S(2)}) async-start(bf16[128,8,256]{0,2,1:T(8,128)(2,1)} %bitcast.3), calls=%async_computation.1 | async-start | bytes 1048576 | tf_op jit(solution)/shard_map/all_to_all | solution.py:154
  31.2 20.7 %all-to-all-start.3 = ((bf16[128,8,256]{0,2,1:T(8,128)(2,1)}), bf16[128,8,256]{0,2,1:T(8,128)(2,1)S(1)}, u32[]{:S(2)}, u32[]{:S(2)}) async-start(bf16[128,8,256]{0,2,1:T(8,128)(2,1)} %bitcast.12), calls=%async_computation.3 | async-start | bytes 1048576 | tf_op jit(solution)/shard_map/all_to_all | solution.py:155
  35.1 4.9 copy-start.11
  36.5 35.5 %collective-permute-start = (bf16[2,896,256]{2,1,0:T(8,128)(2,1)}, bf16[2,896,256]{2,1,0:T(8,128)(2,1)}, u32[]{:S(2)}, u32[]{:S(2)}) collective-permute-start(bf16[2,896,256]{2,1,0:T(8,128)(2,1)} %get-tuple-element.726), channel_id=1, source_target_pairs={{0,8},{8,16},{16,24},{24,32},{32,40},{40,48},{48,56},{56,64},{64,7... | collective-permute-start | bytes 2752520 | tf_op jit(solution)/shard_map/ppermute | solution.py:24
  40.0 32.1 %collective-permute-start.1 = (bf16[2,896,256]{2,1,0:T(8,128)(2,1)}, bf16[2,896,256]{2,1,0:T(8,128)(2,1)}, u32[]{:S(2)}, u32[]{:S(2)}) collective-permute-start(bf16[2,896,256]{2,1,0:T(8,128)(2,1)} %get-tuple-element.727), channel_id=1, source_target_pairs={{8,0},{16,8},{24,16},{32,24},{40,32},{48,40},{56,48},{64,56},{72,6... | collective-permute-start | bytes 2752520 | tf_op jit(solution)/shard_map/ppermute | solution.py:25
  45.3 15.9 %copy-start.5 = (bf16[4096,256]{0,1:T(8,128)(2,1)}, bf16[4096,256]{0,1:T(8,128)(2,1)S(1)}, u32[]{:S(2)}) copy-start(bf16[4096,256]{0,1:T(8,128)(2,1)S(1)} %copy.122) | copy-start | bytes 6291460
  51.9 18.2 %all-to-all-start.2 = ((bf16[128,8,256]{0,2,1:T(8,128)(2,1)}), bf16[128,8,256]{0,2,1:T(8,128)(2,1)}, u32[]{:S(2)}, u32[]{:S(2)}) async-start(bf16[128,8,256]{0,2,1:T(8,128)(2,1)} %bitcast.246), calls=%async_computation.2 | async-start | bytes 1048576 | tf_op jit(solution)/shard_map/all_to_all | solution.py:152
  61.3 293.7 %collective-permute-start.2 = (bf16[2,3584,256]{1,2,0:T(8,128)(2,1)}, bf16[2,3584,256]{1,2,0:T(8,128)(2,1)}, u32[]{:S(2)}, u32[]{:S(2)}) collective-permute-start(bf16[2,3584,256]{1,2,0:T(8,128)(2,1)} %get-tuple-element.720), channel_id=1, source_target_pairs={{0,8},{8,16},{16,24},{24,32},{32,40},{40,48},{48,56},{56,64},{64,7... | collective-permute-start | bytes 11010056 | tf_op jit(solution)/shard_map/ppermute | solution.py:24
  66.9 288.1 %collective-permute-start.3 = (bf16[2,3584,256]{1,2,0:T(8,128)(2,1)}, bf16[2,3584,256]{1,2,0:T(8,128)(2,1)}, u32[]{:S(2)}, u32[]{:S(2)}) collective-permute-start(bf16[2,3584,256]{1,2,0:T(8,128)(2,1)} %get-tuple-element.721), channel_id=1, source_target_pairs={{8,0},{16,8},{24,16},{32,24},{40,32},{48,40},{56,48},{64,56},{72,6... | collective-permute-start | bytes 11010056 | tf_op jit(solution)/shard_map/ppermute | solution.py:25
  76.9 3.5 copy-start.18
  76.9 3.5 copy-start.20
  92.2 4.6 copy-start.8
  93.5 3.3 copy-start.9
  93.5 3.5 copy-start
  125.9 4.6 copy-start.8
  127.2 3.3 copy-start.9
  127.2 3.5 copy-start
  159.5 4.6 copy-start.8
  160.9 3.3 copy-start.9
  160.9 3.5 copy-start
  193.3 4.6 copy-start.8
  194.6 3.3 copy-start.9
  194.6 3.5 copy-start
  227.0 4.6 copy-start.8
  228.3 3.3 copy-start.9
  228.4 3.5 copy-start
  260.7 4.6 copy-start.8
  262.0 3.3 copy-start.9
  262.0 3.5 copy-start
  294.4 4.6 copy-start.8
  295.7 3.3 copy-start.9
  295.8 3.5 copy-start
  328.1 4.6 copy-start.8
  329.4 3.3 copy-start.9
  329.5 3.5 copy-start
  350.2 2.7 copy-start.3
  352.3 2.7 copy-start.6
  352.3 2.7 copy-start.7
  370.2 4.6 copy-start.17
  370.2 4.6 copy-start.19
  370.2 4.6 copy-start.21
  400.1 4.0 copy-start.1
  492.4 4.0 copy-start.1
  584.5 4.0 copy-start.1
  676.6 4.0 copy-start.1
  681.8 1.6 copy-start.2
  768.7 4.0 copy-start.1
  773.9 1.6 copy-start.2
  860.8 4.0 copy-start.1
  952.9 4.0 copy-start.1
  1044.9 4.0 copy-start.1
  1111.9 6.1 slice-start
  1111.9 6.8 slice-start.1
  1111.9 7.7 slice-start.2
  1121.4 8.5 copy-start.12
  1121.4 8.6 copy-start.13
  1123.7 104.9 %collective-permute-start.4 = (bf16[2,4480,256]{2,1,0:T(8,128)(2,1)}, bf16[2,4480,256]{2,1,0:T(8,128)(2,1)}, u32[]{:S(2)}, u32[]{:S(2)}) collective-permute-start(bf16[2,4480,256]{2,1,0:T(8,128)(2,1)} %maximum_maximum_fusion), channel_id=1, source_target_pairs={{0,8},{8,16},{16,24},{24,32},{32,40},{40,48},{48,56},{56,64},{64,7... | collective-permute-start | bytes 13762568 | tf_op jit(solution)/shard_map/ppermute | solution.py:33
  1132.2 104.9 %collective-permute-start.5 = (bf16[2,4480,256]{2,1,0:T(8,128)(2,1)}, bf16[2,4480,256]{2,1,0:T(8,128)(2,1)}, u32[]{:S(2)}, u32[]{:S(2)}) collective-permute-start(bf16[2,4480,256]{2,1,0:T(8,128)(2,1)} %maximum_maximum_fusion.1), channel_id=1, source_target_pairs={{8,0},{16,8},{24,16},{32,24},{40,32},{48,40},{56,48},{64,56},{72,6... | collective-permute-start | bytes 13762568 | tf_op jit(solution)/shard_map/ppermute | solution.py:33
  1149.2 13.8 %all-to-all-start.5 = ((bf16[8,128,256]{1,2,0:T(8,128)(2,1)}), bf16[8,128,256]{1,2,0:T(8,128)(2,1)S(1)}, u32[]{:S(2)}, u32[]{:S(2)}) async-start(bf16[8,128,256]{1,2,0:T(8,128)(2,1)} %get-tuple-element.531), calls=%async_computation.5 | async-start | bytes 1048576 | tf_op jit(solution)/shard_map/all_to_all | solution.py:203
  1240.1 3.5 copy-start.4
  1246.0 14.8 %all-to-all-start.7 = ((bf16[8,128,256]{2,1,0:T(8,128)(2,1)}), bf16[8,128,256]{2,1,0:T(8,128)(2,1)S(1)}, u32[]{:S(2)}, u32[]{:S(2)}) async-start(bf16[8,128,256]{2,1,0:T(8,128)(2,1)} %bitcast.39), calls=%async_computation.7 | async-start | bytes 1048576 | tf_op jit(solution)/shard_map/all_to_all | solution.py:205
  1260.8 15.1 %all-to-all-start.6 = ((bf16[8,128,256]{2,1,0:T(8,128)(2,1)}), bf16[8,128,256]{2,1,0:T(8,128)(2,1)S(1)}, u32[]{:S(2)}, u32[]{:S(2)}) async-start(bf16[8,128,256]{2,1,0:T(8,128)(2,1)} %bitcast.34), calls=%async_computation.6 | async-start | bytes 1048576 | tf_op jit(solution)/shard_map/all_to_all | solution.py:204
  (16 other events, 19.3 us)
where the time goes:
time: 1290 us; the launch traced here: 1280 us
  local copies, waits for them, and re-layouts  619 us (48%)
  matrix products  257 us (20%)
  other arithmetic  179 us (14%)
  waiting for transfers between devices  95 us (7%)
  loops' own time  61.7 us (5%)
  starting transfers between devices  49.1 us (4%)
  blocking collectives  15 us (1%)
    dynamic_slice x64, local copies, waits for them, and re-layouts, add_rows(): current = lax.dynamic_slice_in_dim(full, start, piece.shape[axis], axis)  187 us
    dynamic_update_slice x48, local copies, waits for them, and re-layouts, add_rows(): return lax.dynamic_update_slice_in_dim(full, current + piece, start, axis)  165 us
    add x32, other arithmetic, add_rows(): return lax.dynamic_update_slice_in_dim(full, current + piece, start, axis)  111 us
    slice x16, local copies, waits for them, and re-layouts, step(): near_pair[0]  89.8 us
    dot_general x16, matrix products, attend_tile(): jnp.einsum('grk,rge->kge', weights_half, grad_out, preferred_element_type...  70 us
    ppermute x2, waiting for transfers between devices, shifted(): return lax.ppermute(block, axis, route)  66.5 us
    another operation x2, loops' own time, one_direction(): lax.scan(step, (empty, empty), jnp.arange(count, dtype=jnp.int32))  61.7 us
    sub x16, matrix products, attend_tile(): exponent = jnp.where(key_valid, jnp.exp(scores - row_top), 0.0)  59.2 us
  transfers between devices with their start and end apart: 13, of which 6 were waited for; matrix products, arithmetic and copies ran while one was open for 24% of the time, Pallas kernels for 0%

commit v1 on v0

v1 whole, which is shorter than its diff:
```python
import functools
import math

import jax
import jax.numpy as jnp
from jax import lax
from jax.experimental import pallas as pl
from jax.experimental.pallas import tpu as pltpu
from jax.sharding import PartitionSpec as P

DH = 128
BV = 512
BA = 128
P_SIZE = 8
NB = 128
SPAN = 8
REACH = P_SIZE - 1
EXT = SPAN + 2 * REACH
WIDE = 2 * DH
NEG = -1e30
INV_ROOT = 1.0 / math.sqrt(DH)
C2 = math.log2(math.e) / math.sqrt(DH)
F32 = jnp.float32
BF16 = jnp.bfloat16
MIB = 1024 * 1024
PACK = 16
GROUP_FORMS = (5, 6, 8)
VIDEO_ROWS = SPAN * BV
AUDIO_ROWS = EXT * BA


def dot_nt(a, b):
    return lax.dot_general(a, b, (((1,), (1,)), ((), ())), preferred_element_type=F32)


def dot_nn(a, b):
    return jnp.dot(a, b, preferred_element_type=F32)


def split_rows(column0, column1, rows):
    return jnp.concatenate(
        [jnp.broadcast_to(column0, (rows, DH)), jnp.broadcast_to(column1, (rows, DH))], axis=1
    )


def put_diagonal(ref, tile):
    ref[0:DH, 0:DH] = tile[:, 0:DH]
    ref[DH:WIDE, DH:WIDE] = tile[:, DH:WIDE]


def clear_corners(ref):
    ref[0:DH, DH:WIDE] = jnp.zeros((DH, DH), ref.dtype)
    ref[DH:WIDE, 0:DH] = jnp.zeros((DH, DH), ref.dtype)


def padded(length):
    return (length + PACK - 1) // PACK * PACK


def aligned(row):
    return pl.multiple_of(row, PACK)


def pick(cond, value, other):
    return jnp.where(cond, value, other)


def block_row(count, width):
    return lax.broadcasted_iota(jnp.int32, (count, width), 0)


def global_block(first, e):
    return jnp.clip(first - REACH + e, 0, NB - 1)


def pack_kernel(first_ref, len_ref, k_ref, v_ref, kc_ref, vc_ref):
    first = first_ref[0]
    row = block_row(BV, WIDE)
    zeros = jnp.zeros((BV, WIDE), BF16)

    def one(c, offset):
        length = len_ref[first + c]
        rows = pl.ds(aligned(offset), BV)
        kc_ref[rows, :] = pick(row < length, k_ref[c], zeros)
        vc_ref[rows, :] = pick(row < length, v_ref[c], zeros)
        return offset + padded(length)

    end = lax.fori_loop(0, SPAN, one, 0)
    rows = pl.ds(aligned(end), BV)
    kc_ref[rows, :] = zeros
    vc_ref[rows, :] = zeros


def run_pack(first, lengths, k, v):
    shape = (VIDEO_ROWS + BV, WIDE)
    return pl.pallas_call(
        pack_kernel,
        grid_spec=pltpu.PrefetchScalarGridSpec(
            num_scalar_prefetch=2,
            grid=(1,),
            in_specs=[whole(k.shape), whole(v.shape)],
            out_specs=[whole(shape), whole(shape)],
        ),
        out_shape=[jax.ShapeDtypeStruct(shape, BF16)] * 2,
        compiler_params=pltpu.CompilerParams(vmem_limit_bytes=12 * MIB),
        cost_estimate=pl.CostEstimate(
            flops=1_000_000_000, bytes_accessed=20_000_000, transcendentals=0
        ),
        name="pack_video",
    )(first, lengths, k, v)


def video_kernel(
    first_ref,
    pairs_ref,
    len_ref,
    q_ref,
    do_ref,
    before_ref,
    own_ref,
    after_ref,
    out_ref,
    dq_ref,
    gbefore_ref,
    gown_ref,
    gafter_ref,
    kc,
    vc,
    bias,
    dk_acc,
    dv_acc,
    kbd,
    vbd,
    s_scr,
    p_scr,
    offsets,
):
    j = pl.program_id(0)
    first = first_ref[0]
    sources = (
        (before_ref, gbefore_ref, 0, REACH),
        (own_ref, gown_ref, REACH, SPAN),
        (after_ref, gafter_ref, REACH + SPAN, REACH),
    )
    row = block_row(BA, WIDE)
    narrow_row = block_row(BA, BA)

    @pl.when(j == 0)
    def _():
        for i in range(P_SIZE):
            clear_corners(kbd.at[i])
            clear_corners(vbd.at[i])

        def clear(i, carry):
            rows = pl.ds(i * BA, BA)
            kc[rows, :] = jnp.zeros((BA, WIDE), BF16)
            vc[rows, :] = jnp.zeros((BA, WIDE), BF16)
            bias[rows, :] = jnp.full((BA, BA), NEG, F32)
            dk_acc[rows, :] = jnp.zeros((BA, WIDE), F32)
            dv_acc[rows, :] = jnp.zeros((BA, WIDE), F32)
            return carry

        lax.fori_loop(0, EXT + 1, clear, 0)
        offset = jnp.int32(0)
        for source, _, base, count in sources:

            def one(i, offset, source=source, base=base):
                length = len_ref[global_block(first, base + i)]
                rows = pl.ds(aligned(offset), BA)
                offsets[base + i] = offset
                kc[rows, :] = pick(row < length, source[i, 0], jnp.zeros((BA, WIDE), BF16))
                vc[rows, :] = pick(row < length, source[i, 1], jnp.zeros((BA, WIDE), BF16))
                bias[rows, :] = pick(narrow_row < length, 0.0, NEG)
                return offset + padded(length)

            offset = lax.fori_loop(0, count, one, offset)
        offsets[EXT] = offset

    start = pairs_ref[first + j, 0]
    e = start - first + REACH
    low = offsets[e]
    high = offsets[e + P_SIZE]
    groups = (high - low + BA - 1) // BA
    place = lax.broadcasted_iota(jnp.int32, (BA, BA), 1)

    def attend(count):
        q = q_ref[...]
        do = do_ref[...]
        spots = []
        for i in range(count):
            begin = jnp.minimum(low + i * BA, AUDIO_ROWS)
            rows = pl.ds(aligned(begin), BA)
            spots.append(rows)
            put_diagonal(kbd.at[i], kc[rows, :])
            put_diagonal(vbd.at[i], vc[rows, :])
        top = None
        for i in range(count):
            begin = jnp.minimum(low + i * BA, AUDIO_ROWS)
            shut = pick(place < high - begin, bias[spots[i], :].T, NEG)[0:1, :]
            s = dot_nt(q, kbd[i]) + jnp.concatenate([shut, shut], axis=1)
            s_scr[i] = s
            top = s if top is None else jnp.maximum(top, s)
        peak = C2 * split_rows(
            jnp.max(top[:, 0:DH], axis=1, keepdims=True),
            jnp.max(top[:, DH:WIDE], axis=1, keepdims=True),
            BV,
        )
        total = None
        acc = None
        for i in range(count):
            ex = jnp.exp2(s_scr[i] * C2 - peak)
            total = ex if total is None else total + ex
            p = ex.astype(BF16)
            p_scr[i] = p
            part = dot_nn(p, vbd[i])
            acc = part if acc is None else acc + part
        scale = 1.0 / split_rows(
            jnp.sum(total[:, 0:DH], axis=1, keepdims=True),
            jnp.sum(total[:, DH:WIDE], axis=1, keepdims=True),
            BV,
        )
        out = acc * scale
        out_ref[...] = out.astype(BF16)
        do_wide = do.astype(F32)
        prod = do_wide * out
        delta = split_rows(
            jnp.sum(prod[:, 0:DH], axis=1, keepdims=True),
            jnp.sum(prod[:, DH:WIDE], axis=1, keepdims=True),
            BV,
        )
        scale_in = scale * INV_ROOT
        q_t = (q.astype(F32) * scale_in).astype(BF16).T
        do_t = (do_wide * scale).astype(BF16).T
        acc = None
        for i in range(count):
            dp = dot_nt(do, vbd[i])
            p = p_scr[i]
            ds = (p.astype(F32) * (dp - delta)).astype(BF16)
            part = dot_nn(ds, kbd[i])
            acc = part if acc is None else acc + part
            for h in range(2):
                cut = slice(h * DH, (h + 1) * DH)
                dk_acc[spots[i], cut] += dot_nn(q_t[cut, :], ds[:, cut]).T
                dv_acc[spots[i], cut] += dot_nn(do_t[cut, :], p[:, cut]).T
        dq_ref[...] = (acc * scale_in).astype(BF16)

    below = 0
    for count in GROUP_FORMS:
        pl.when(jnp.logical_and(groups > below, groups <= count))(functools.partial(attend, count))
        below = count

    @pl.when(j == pl.num_programs(0) - 1)
    def _():
        for _, target, base, count in sources:

            def one(i, carry, target=target, base=base):
                length = len_ref[global_block(first, base + i)]
                rows = pl.ds(aligned(offsets[base + i]), BA)
                target[i, 0] = pick(row < length, dk_acc[rows, :], 0.0).astype(target.dtype)
                target[i, 1] = pick(row < length, dv_acc[rows, :], 0.0).astype(target.dtype)
                return carry

            lax.fori_loop(0, count, one, 0)


def whole(shape):
    return pl.BlockSpec(shape, lambda *_: (0,) * len(shape), pipeline_mode=pl.Buffered(1))


def run_video(first, pairs, lengths, q, do, before, own, after):
    rows = pl.BlockSpec((BV, WIDE), lambda j, *_: (j, 0))
    return pl.pallas_call(
        video_kernel,
        grid_spec=pltpu.PrefetchScalarGridSpec(
            num_scalar_prefetch=3,
            grid=(SPAN,),
            in_specs=[rows, rows, whole(before.shape), whole(own.shape), whole(after.shape)],
            out_specs=[rows, rows, whole(before.shape), whole(own.shape), whole(after.shape)],
            scratch_shapes=[
                pltpu.VMEM((AUDIO_ROWS + BA, WIDE), BF16),
                pltpu.VMEM((AUDIO_ROWS + BA, WIDE), BF16),
                pltpu.VMEM((AUDIO_ROWS + BA, BA), F32),
                pltpu.VMEM((AUDIO_ROWS + BA, WIDE), F32),
                pltpu.VMEM((AUDIO_ROWS + BA, WIDE), F32),
                pltpu.VMEM((P_SIZE, WIDE, WIDE), BF16),
                pltpu.VMEM((P_SIZE, WIDE, WIDE), BF16),
                pltpu.VMEM((P_SIZE, BV, WIDE), F32),
                pltpu.VMEM((P_SIZE, BV, WIDE), BF16),
                pltpu.SMEM((32,), jnp.int32),
            ],
        ),
        out_shape=[
            jax.ShapeDtypeStruct(q.shape, BF16),
            jax.ShapeDtypeStruct(q.shape, BF16),
            jax.ShapeDtypeStruct(before.shape, BF16),
            jax.ShapeDtypeStruct(own.shape, F32),
            jax.ShapeDtypeStruct(after.shape, BF16),
        ],
        compiler_params=pltpu.CompilerParams(vmem_limit_bytes=32 * MIB),
        cost_estimate=pl.CostEstimate(
            flops=20_000_000_000, bytes_accessed=20_000_000, transcendentals=8_000_000
        ),
        name="video_queries",
    )(first, pairs, lengths, q, do, before, own, after)


def packed_range(first, pairs_ref, offsets, block):
    inside = jnp.logical_and(block >= 0, block < NB)
    start = pairs_ref[jnp.clip(block, 0, NB - 1), 0] - first
    low = offsets[jnp.clip(start, 0, SPAN)]
    high = offsets[jnp.clip(start + P_SIZE, 0, SPAN)]
    return low, pick(inside, high, low)


def fill_bias(first, len_ref, bias, offsets):
    row = block_row(BV, BA)

    def one(c, offset):
        length = len_ref[first + c]
        offsets[c] = offset
        bias[pl.ds(aligned(offset), BV), :] = pick(row < length, 0.0, NEG)
        return offset + padded(length)

    end = lax.fori_loop(0, SPAN, one, 0)
    offsets[SPAN] = end
    bias[pl.ds(aligned(end), BV), :] = jnp.full((BV, BA), NEG, F32)


def part_kernel(pieces, first_ref, pairs_ref, len_ref, *refs):
    sources = refs[: len(pieces)]
    kc_ref, vc_ref, o_ref, st_ref, qbd, s_scr, bias, offsets = refs[len(pieces) :]
    b = pl.program_id(0)
    first = first_ref[0]

    @pl.when(b == 0)
    def _():
        clear_corners(qbd)
        fill_bias(first, len_ref, bias, offsets)

    block = first
    for base, begin, count in pieces:
        inside = jnp.logical_and(b >= begin, b < begin + count)
        block = pick(inside, first + base + b - begin, block)
    low, high = packed_range(first, pairs_ref, offsets, block)
    chunks = (high - low + BV - 1) // BV
    row = block_row(BV, BA)

    @pl.when(chunks == 0)
    def _():
        o_ref[0] = jnp.zeros((WIDE, BA), F32)
        st_ref[0, 0:1, :] = jnp.full((1, WIDE), NEG, F32)
        st_ref[0, 1:2, :] = jnp.zeros((1, WIDE), F32)

    for (_, begin, count), source in zip(pieces, sources):

        @pl.when(jnp.logical_and(chunks > 0, jnp.logical_and(b >= begin, b < begin + count)))
        def _(source=source, begin=begin):
            put_diagonal(qbd, source[b - begin, 0])

    def attend(count):
        spots = [aligned(low + i * BV) for i in range(count)]
        peak = None
        for i, spot in enumerate(spots):
            rows = pl.ds(spot, BV)
            shut = bias[rows, :]
            if i == count - 1:
                shut = pick(row < high - spot, shut, NEG)
            s = dot_nt(kc_ref[rows, :], qbd[...]) + jnp.concatenate([shut, shut], axis=1)
            s_scr[i] = s
            top = jnp.max(s, axis=0, keepdims=True)
            peak = top if peak is None else jnp.maximum(peak, top)
        peak = peak * C2
        total = None
        acc = [None, None]
        for i, spot in enumerate(spots):
            ex = jnp.exp2(s_scr[i] * C2 - peak)
            part = jnp.sum(ex, axis=0, keepdims=True)
            total = part if total is None else total + part
            p = ex.astype(BF16)
            v_t = vc_ref[pl.ds(spot, BV), :].T
            for h in range(2):
                cut = slice(h * DH, (h + 1) * DH)
                part = dot_nn(v_t[cut, :], p[:, cut])
                acc[h] = part if acc[h] is None else acc[h] + part
        scale = 1.0 / total
        st_ref[0, 0:1, :] = peak + jnp.log2(total)
        for h in range(2):
            cut = slice(h * DH, (h + 1) * DH)
            o_ref[0, cut, :] = acc[h] * scale[:, cut]

    for count in range(1, SPAN + 1):
        pl.when(chunks == count)(functools.partial(attend, count))

    for (_, begin, count), source in zip(pieces, sources):

        @pl.when(jnp.logical_and(chunks > 0, jnp.logical_and(b >= begin, b < begin + count)))
        def _(source=source, begin=begin):
            for h in range(2):
                cut = slice(h * DH, (h + 1) * DH)
                do_t = source[b - begin, 1, :, cut].T.astype(F32)
                st_ref[0, 1:2, cut] = jnp.sum(o_ref[0, cut, :] * do_t, axis=0, keepdims=True)


def run_part(pieces, first, pairs, lengths, sources, kc, vc):
    count = sum(piece[2] for piece in pieces)
    return pl.pallas_call(
        functools.partial(part_kernel, pieces),
        grid_spec=pltpu.PrefetchScalarGridSpec(
            num_scalar_prefetch=3,
            grid=(count,),
            in_specs=[whole(a.shape) for a in sources] + [whole(kc.shape), whole(vc.shape)],
            out_specs=[
                pl.BlockSpec((1, WIDE, BA), lambda b, *_: (b, 0, 0)),
                pl.BlockSpec((1, 8, WIDE), lambda b, *_: (b, 0, 0)),
            ],
            scratch_shapes=[
                pltpu.VMEM((WIDE, WIDE), BF16),
                pltpu.VMEM((SPAN, BV, WIDE), F32),
                pltpu.VMEM((VIDEO_ROWS + BV, BA), F32),
                pltpu.SMEM((16,), jnp.int32),
            ],
        ),
        out_shape=[
            jax.ShapeDtypeStruct((count, WIDE, BA), F32),
            jax.ShapeDtypeStruct((count, 8, WIDE), F32),
        ],
        compiler_params=pltpu.CompilerParams(vmem_limit_bytes=18 * MIB),
        cost_estimate=pl.CostEstimate(
            flops=8_000_000_000, bytes_accessed=6_000_000, transcendentals=count * 500_000
        ),
        name="audio_parts",
    )(first, pairs, lengths, *sources, kc, vc)


def grad_kernel(pieces, last, first_ref, pairs_ref, len_ref, *refs):
    n = len(pieces)
    sources = refs[:n]
    rest = refs[n:]
    st_ref, above_ref, below_ref, o_ref, kc_ref, vc_ref = rest[:6]
    rest = rest[6:]
    if last:
        dk_in, dv_in = rest[:2]
        rest = rest[2:]
    targets = rest[:n]
    dk_ref, dv_ref, qbd, dobd, acc, bias, offsets = rest[n : n + 7]
    if last:
        dk_acc, dv_acc = rest[n + 7 :]
    else:
        dk_acc, dv_acc = dk_ref, dv_ref
    b = pl.program_id(0)
    first = first_ref[0]

    @pl.when(b == 0)
    def _():
        clear_corners(qbd)
        clear_corners(dobd)
        fill_bias(first, len_ref, bias, offsets)

        def clear(c, carry):
            rows = pl.ds(pl.multiple_of(c * BV, BV), BV)
            dk_acc[rows, :] = dk_in[rows, :] if last else jnp.zeros((BV, WIDE), F32)
            dv_acc[rows, :] = dv_in[rows, :] if last else jnp.zeros((BV, WIDE), F32)
            return carry

        lax.fori_loop(0, SPAN + 1, clear, 0)

    block = first
    for base, begin, count in pieces:
        inside = jnp.logical_and(b >= begin, b < begin + count)
        block = pick(inside, first + base + b - begin, block)
    low, high = packed_range(first, pairs_ref, offsets, block)
    chunks = (high - low + BV - 1) // BV
    row = block_row(BV, BA)
    for (_, begin, count), source, target in zip(pieces, sources, targets):
        inside = jnp.logical_and(b >= begin, b < begin + count)

        @pl.when(jnp.logical_and(chunks > 0, inside))
        def _(source=source, begin=begin):
            put_diagonal(qbd, source[b - begin, 0])
            put_diagonal(dobd, source[b - begin, 1])

        @pl.when(jnp.logical_and(chunks == 0, inside))
        def _(target=target, begin=begin):
            target[b - begin] = jnp.zeros((2, BA, WIDE), target.dtype)

    mine = st_ref[b]
    if last:
        above = above_ref[REACH + jnp.maximum(b - 1, 0)]
        below = below_ref[REACH + jnp.minimum(b, REACH - 1)]
        logs = [
            mine[0:1],
            pick(b >= 1, above[0:1], NEG),
            pick(b < REACH, below[0:1], NEG),
        ]
        parts = [mine[1:2], above[1:2], below[1:2]]
    else:
        is_before = b < REACH
        slot = pick(is_before, b, b - REACH)
        other = pick(is_before, below_ref[slot], above_ref[slot])
        logs = [mine[0:1], other[0:1]]
        parts = [mine[1:2], other[1:2]]
    peak = functools.reduce(jnp.maximum, logs)
    log_total = peak + jnp.log2(sum(jnp.exp2(x - peak) for x in logs))
    shares = [jnp.exp2(x - log_total) for x in logs]
    delta = sum(x * y for x, y in zip(shares, parts))

    @pl.when(chunks > 0)
    def _():
        acc[...] = jnp.zeros((WIDE, BA), F32)

    def step(i, carry):
        begin = aligned(low + i * BV)
        rows = pl.ds(begin, BV)
        shut = pick(row < high - begin, bias[rows, :], NEG)
        k = kc_ref[rows, :]
        s = dot_nt(k, qbd[...])
        w = jnp.exp2(s * C2 - log_total + jnp.concatenate([shut, shut], axis=1))
        dp = dot_nt(vc_ref[rows, :], dobd[...])
        ds = (w * (dp - delta)).astype(BF16)
        w = w.astype(BF16)
        dv_acc[rows, :] += dot_nn(w, dobd[...])
        dk_acc[rows, :] += dot_nn(ds, qbd[...])
        k_t = k.T
        for h in range(2):
            cut = slice(h * DH, (h + 1) * DH)
            acc[cut, :] += dot_nn(k_t[cut, :], ds[:, cut])
        return carry

    lax.fori_loop(0, chunks, step, 0)
    for (_, begin, count), target in zip(pieces, targets):

        @pl.when(jnp.logical_and(chunks > 0, jnp.logical_and(b >= begin, b < begin + count)))
        def _(target=target, begin=begin):
            for h in range(2):
                cut = slice(h * DH, (h + 1) * DH)
                spread = (o_ref[0, cut, :] * shares[0][:, cut]).T
                target[b - begin, 0, :, cut] = spread.astype(target.dtype)
                target[b - begin, 1, :, cut] = (acc[cut, :].T * INV_ROOT).astype(target.dtype)

    if last:

        @pl.when(b == pl.num_programs(0) - 1)
        def _():
            full_row = block_row(BV, WIDE)

            def drain(c, offset):
                length = len_ref[first + c]
                rows = pl.ds(aligned(offset), BV)
                valid = full_row < length
                dk_ref[c] = (pick(valid, dk_acc[rows, :], 0.0) * INV_ROOT).astype(BF16)
                dv_ref[c] = pick(valid, dv_acc[rows, :], 0.0).astype(BF16)
                return offset + padded(length)

            lax.fori_loop(0, SPAN, drain, 0)


def run_grad(pieces, last, first, pairs, lengths, sources, stats, above, below, o_t, kc, vc, accs):
    count = sum(piece[2] for piece in pieces)
    acc_shape = kc.shape
    grad_shape = (SPAN, BV, WIDE) if last else acc_shape
    target_shapes = [(piece[2], 2, BA, WIDE) for piece in pieces]
    operands = (*sources, stats, above, below, o_t, kc, vc, *accs)
    in_specs = [whole(a.shape) for a in operands]
    in_specs[len(sources) + 3] = pl.BlockSpec((1, WIDE, BA), lambda b, *_: (b, 0, 0))
    scratch = [
        pltpu.VMEM((WIDE, WIDE), BF16),
        pltpu.VMEM((WIDE, WIDE), BF16),
        pltpu.VMEM((WIDE, BA), F32),
        pltpu.VMEM((VIDEO_ROWS + BV, BA), F32),
        pltpu.SMEM((16,), jnp.int32),
    ]
    if last:
        scratch += [pltpu.VMEM(acc_shape, F32), pltpu.VMEM(acc_shape, F32)]
    return pl.pallas_call(
        functools.partial(grad_kernel, pieces, last),
        grid_spec=pltpu.PrefetchScalarGridSpec(
            num_scalar_prefetch=3,
            grid=(count,),
            in_specs=in_specs,
            out_specs=[whole(x) for x in target_shapes] + [whole(grad_shape)] * 2,
            scratch_shapes=scratch,
        ),
        out_shape=[jax.ShapeDtypeStruct(x, F32 if last else BF16) for x in target_shapes]
        + [jax.ShapeDtypeStruct(grad_shape, BF16 if last else F32)] * 2,
        compiler_params=pltpu.CompilerParams(vmem_limit_bytes=32 * MIB),
        cost_estimate=pl.CostEstimate(
            flops=10_000_000_000, bytes_accessed=20_000_000, transcendentals=4_000_000
        ),
        name="audio_gradients",
    )(first, pairs, lengths, *operands)


def routes(ring):
    size = lax.axis_size("vid")
    count = size if ring else size - 1
    up = [(i, (i + 1) % size) for i in range(count)]
    return up, [(j, i) for i, j in up]


def to_span(*arrays):
    tiles = jnp.stack([a.reshape(BA, 8, WIDE) for a in arrays], axis=1)
    tiles = jnp.transpose(tiles, (2, 1, 0, 3))
    return lax.all_to_all(tiles, "aud", split_axis=0, concat_axis=0, tiled=True)


def to_owner(tiles):
    back = lax.all_to_all(tiles, "aud", split_axis=0, concat_axis=0, tiled=True)
    return [jnp.transpose(back[:, i], (1, 0, 2)).reshape(BA, 8 * WIDE) for i in range(2)]


def halo(tiles):
    up, down = routes(False)
    return lax.ppermute(tiles[1:], "vid", up), lax.ppermute(tiles[:-1], "vid", down)


def give_back(before, after):
    up, down = routes(False)
    return lax.ppermute(before, "vid", down), lax.ppermute(after, "vid", up)


def spread_low(part):
    return jnp.pad(part, ((0, 1),) + ((0, 0),) * (part.ndim - 1))


def spread_high(part):
    return jnp.pad(part, ((1, 0),) + ((0, 0),) * (part.ndim - 1))


OWN = ((0, 0, SPAN),)
HALO = ((-REACH, 0, REACH), (SPAN, REACH, REACH))


def per_device(
    video_q,
    video_k,
    video_v,
    video_dout,
    audio_q,
    audio_k,
    audio_v,
    audio_dout,
    video_pairs,
    audio_pairs,
    video_len,
    audio_len,
):
    first = (lax.axis_index("vid") * SPAN).astype(jnp.int32).reshape(1)
    k = video_k.reshape(SPAN, BV, WIDE)
    v = video_v.reshape(SPAN, BV, WIDE)
    kc, vc = run_pack(first, video_len, k, v)
    qd = to_span(audio_q, audio_dout)
    qd, kc, vc = lax.optimization_barrier((qd, kc, vc))
    qd_before, qd_after = halo(qd)
    kv = to_span(audio_k, audio_v)
    kv_before, kv_after = halo(kv)

    o_own, st_own = run_part(OWN, first, audio_pairs, video_len, (qd,), kc, vc)
    near = (qd_before, qd_after)
    o_near, st_near = run_part(HALO, first, audio_pairs, video_len, near, kc, vc)
    up, down = routes(True)
    from_above = lax.ppermute(jnp.concatenate([st_own[:-1], st_near[:REACH]]), "vid", down)
    from_below = lax.ppermute(jnp.concatenate([st_own[1:], st_near[REACH:]]), "vid", up)

    video_out, video_dq, g_before, g_own, g_after = run_video(
        first, video_pairs, audio_len, video_q, video_dout, kv_before, kv, kv_after
    )
    g_above, g_below = give_back(g_before, g_after)

    od_before, od_after, dk_acc, dv_acc = run_grad(
        HALO, False, first, audio_pairs, video_len, near, st_near, from_above, from_below, o_near, kc, vc, ()
    )
    od_above, od_below = give_back(od_before, od_after)
    od_own, video_dk, video_dv = run_grad(
        OWN, True, first, audio_pairs, video_len, (qd,), st_own, from_above, from_below, o_own, kc, vc,
        (dk_acc, dv_acc),
    )

    g = (g_own + spread_high(g_above).astype(F32) + spread_low(g_below).astype(F32)).astype(BF16)
    audio_dk, audio_dv = to_owner(g)
    od = (od_own + spread_high(od_above).astype(F32) + spread_low(od_below).astype(F32)).astype(BF16)
    audio_out, audio_dq = to_owner(od)
    return (
        video_out,
        audio_out,
        video_dq,
        video_dk.reshape(video_k.shape),
        video_dv.reshape(video_k.shape),
        audio_dq,
        audio_dk,
        audio_dv,
    )


def solution(mesh):
    video = P("vid", "aud")
    audio = P(("vid", "aud"), None)
    return jax.shard_map(
        per_device,
        mesh=mesh,
        in_specs=(video,) * 4 + (audio,) * 4 + (P(),) * 4,
        out_specs=(video, audio, video, video, video, audio, audio, audio),
        check_vma=False,
    )
```

time: 1290 us -> 237 us (0.18)
  local copies, waits for them, and re-layouts: 619 us -> 32.4 us
  matrix products: 257 us -> 0 us
  other arithmetic: 179 us -> 6.18 us
  Pallas kernels: 0 us -> 113 us
  loops' own time: 61.7 us -> 0 us
  waiting for transfers between devices: 95 us -> 34.2 us
  blocking collectives: 15 us -> 0 us
    dynamic_slice x208 -> x0, local copies, waits for them, and re-layouts: 274 us -> none  [the longest x64 187 us: add_rows(): current = lax.dynamic_slice_in_dim(full, start, piece.shape[axis], axis)]
    dot_general x80 -> x0, matrix products: 198 us -> none  [the longest x16 70 us: attend_tile(): jnp.einsum('grk,rge->kge', weights_half, grad_out, preferred_element_type...]
    dynamic_update_slice x80 -> x0, local copies, waits for them, and re-layouts: 179 us -> none  [the longest x48 165 us: add_rows(): return lax.dynamic_update_slice_in_dim(full, current + piece, start, axis)]
    pallas_call x0 -> x6, Pallas kernels: none -> 113 us  [the longest x1 43.7 us: run_video(): pl.pallas_call(video_kernel, grid_spec=pltpu.PrefetchScalarGridSpec(num_s...]
    add x32 -> x0, other arithmetic: 111 us -> none  [add_rows(): return lax.dynamic_update_slice_in_dim(full, current + piece, start, axis)]
    slice x32 -> x3, local copies, waits for them, and re-layouts: 97.8 us -> 1.83 us  [the longest x2 1.81 us: halo(): tiles[:-1]]
    another operation x2 -> x0, loops' own time: 61.7 us -> none  [one_direction(): lax.scan(step, (empty, empty), jnp.arange(count, dtype=jnp.int32))]
    ppermute x6 -> x10, waiting for transfers between devices: 66.5 us -> 5.83 us  [the longest x2 5.81 us: halo(): lax.ppermute(tiles[:-1], 'vid', down)]
  transfers between devices with their start and end apart: 13 -> 14, of which waited for: 6 -> 4; matrix products, arithmetic and copies ran while one was open for 24% -> 5% of each run, Pallas kernels for 0% -> 48%
where the time goes in v1:
time: 237 us; the launch traced here: 235 us
  Pallas kernels  113 us (48%)
  starting transfers between devices  47.6 us (20%)
  waiting for transfers between devices  34.2 us (14%)
  local copies, waits for them, and re-layouts  32.4 us (14%)
  other arithmetic  6.18 us (3%)
    pallas_call x1, Pallas kernels, run_video(): pl.pallas_call(video_kernel, grid_spec=pltpu.PrefetchScalarGridSpec(num_s...  43.7 us
    pallas_call x2, Pallas kernels, run_grad(): pl.pallas_call(functools.partial(grad_kernel, pieces, last), grid_spec=pl...  43.3 us
    unnamed x56, local copies, waits for them, and re-layouts  27.2 us
    pallas_call x2, Pallas kernels, run_part(): pl.pallas_call(functools.partial(part_kernel, pieces), grid_spec=pltpu.Pr...  25.3 us
    all_to_all x2, waiting for transfers between devices, to_span(): return lax.all_to_all(tiles, 'aud', split_axis=0, concat_axis=0, tiled=True)  16.2 us
    ppermute x4, starting transfers between devices, give_back(): return (lax.ppermute(before, 'vid', down), lax.ppermute(after, 'vid', up))  15.9 us
    all_to_all x2, waiting for transfers between devices, to_owner(): back = lax.all_to_all(tiles, 'aud', split_axis=0, concat_axis=0, tiled=True)  12.1 us
    all_to_all x2, starting transfers between devices, to_owner(): back = lax.all_to_all(tiles, 'aud', split_axis=0, concat_axis=0, tiled=True)  9.5 us
  transfers between devices with their start and end apart: 14, of which 4 were waited for; matrix products, arithmetic and copies ran while one was open for 5% of the time, Pallas kernels for 48%

profile of v1, /device:TPU:24, one launch (start us, length us, event | category | flops | bytes accessed | tf_op | source)
XLA Modules:
  0.0 234.9 jit_solution(9146679488554457607)
XLA Ops:
  0.6 1.4 copy.30
  2.0 0.2 copy.32
  2.2 0.3 copy.31
  2.5 0.2 copy.33
  2.8 1.1 maximum_bitcast_fusion.1
  3.8 4.4 %all-to-all-start.1 = ((bf16[8,2,128,256]{3,2,1,0:T(8,128)(2,1)}), bf16[8,2,128,256]{3,2,1,0:T(8,128)(2,1)S(1)}, u32[]{:S(2)}, u32[]{:S(2)}) async-start(bf16[8,2,128,256]{3,2,1,0:T(8,128)(2,1)} %maximum_bitcast_fusion.1), calls=%async_computation.1 | async-start | bytes 2097152 | tf_op jit(solution)/shard_map/all_to_all | solution.py:603
  8.3 0.3 copy.25
  8.5 0.2 copy.27
  8.8 0.3 copy.26
  9.1 0.2 copy.28
  9.3 0.0 copy-start.22
  9.3 0.0 copy-start.2
  9.3 1.1 maximum_bitcast_fusion
  10.4 13.9 %all-to-all-done.1.refs_0_ = bf16[8,2,128,256]{3,2,1,0:T(8,128)(2,1)S(1)} async-done(((bf16[8,2,128,256]{3,2,1,0:T(8,128)(2,1)}), bf16[8,2,128,256]{3,2,1,0:T(8,128)(2,1)S(1)}, u32[]{:S(2)}, u32[]{:S(2)}) %all-to-all-start.1) | async-done | bytes 1048608 | tf_op jit(solution)/shard_map/all_to_all | solution.py:603
  24.2 3.6 %all-to-all-start = ((bf16[8,2,128,256]{3,2,1,0:T(8,128)(2,1)}), bf16[8,2,128,256]{3,2,1,0:T(8,128)(2,1)S(1)}, u32[]{:S(2)}, u32[]{:S(2)}) async-start(bf16[8,2,128,256]{3,2,1,0:T(8,128)(2,1)} %maximum_bitcast_fusion), calls=%async_computation | async-start | bytes 2097152 | tf_op jit(solution)/shard_map/all_to_all | solution.py:603
  27.8 0.1 copy.37.pairs_ref
  27.9 0.1 copy.29.pairs_ref
  28.0 1.6 copy-done
  29.6 1.6 copy-done.1
  31.2 1.1 pack_video.1
  32.4 1.4 copy-done.3
  33.7 1.7 fusion
  35.4 3.5 %collective-permute-start.2 = (bf16[7,2,128,256]{3,2,1,0:T(8,128)(2,1)}, bf16[7,2,128,256]{3,2,1,0:T(8,128)(2,1)S(1)}, u32[]{:S(2)}, u32[]{:S(2)}) collective-permute-start(bf16[7,2,128,256]{3,2,1,0:T(8,128)(2,1)} %get-tuple-element.63), channel_id=1, source_target_pairs={{0,8},{8,16},{16,24},{24,32},{32,40},{40,48},{48,56},{56,64},{64,7... | collective-permute-start | bytes 2752520 | tf_op jit(solution)/shard_map/ppermute | solution.py:613
  39.0 2.4 %collective-permute-start.3 = (bf16[7,2,128,256]{3,2,1,0:T(8,128)(2,1)}, bf16[7,2,128,256]{3,2,1,0:T(8,128)(2,1)}, u32[]{:S(2)}, u32[]{:S(2)}) collective-permute-start(bf16[7,2,128,256]{3,2,1,0:T(8,128)(2,1)} %get-tuple-element.62), channel_id=1, source_target_pairs={{8,0},{16,8},{24,16},{32,24},{40,32},{48,40},{56,48},{64,56},{72,6... | collective-permute-start | bytes 2752520 | tf_op jit(solution)/shard_map/ppermute | solution.py:613
  41.3 2.4 %all-to-all-done.own_ref = bf16[8,2,128,256]{3,2,1,0:T(8,128)(2,1)S(1)} async-done(((bf16[8,2,128,256]{3,2,1,0:T(8,128)(2,1)}), bf16[8,2,128,256]{3,2,1,0:T(8,128)(2,1)S(1)}, u32[]{:S(2)}, u32[]{:S(2)}) %all-to-all-start) | async-done | bytes 1048608 | tf_op jit(solution)/shard_map/all_to_all | solution.py:603
  43.7 0.1 fusion.1
  43.8 3.6 %collective-permute-start = (bf16[7,2,128,256]{3,2,1,0:T(8,128)(2,1)S(1)}, bf16[7,2,128,256]{3,2,1,0:T(8,128)(2,1)S(1)}, u32[]{:S(2)}, u32[]{:S(2)}) collective-permute-start(bf16[7,2,128,256]{3,2,1,0:T(8,128)(2,1)S(1)} %get-tuple-element.65), channel_id=1, source_target_pairs={{0,8},{8,16},{16,24},{24,32},{32,40},{40,48},{48,56},{56,64},{64,7... | collective-permute-start | bytes 2752520 | tf_op jit(solution)/shard_map/ppermute | solution.py:613
  47.4 2.5 %collective-permute-start.1 = (bf16[7,2,128,256]{3,2,1,0:T(8,128)(2,1)S(1)}, bf16[7,2,128,256]{3,2,1,0:T(8,128)(2,1)S(1)}, u32[]{:S(2)}, u32[]{:S(2)}) collective-permute-start(bf16[7,2,128,256]{3,2,1,0:T(8,128)(2,1)S(1)} %get-tuple-element.64), channel_id=1, source_target_pairs={{8,0},{16,8},{24,16},{32,24},{40,32},{48,40},{56,48},{64,56},{72,6... | collective-permute-start | bytes 2752520 | tf_op jit(solution)/shard_map/ppermute | solution.py:613
  50.0 1.7 copy-done.7
  51.6 15.7 %audio_parts.2 = (f32[8,256,128]{2,1,0:T(8,128)S(1)}, f32[8,8,256]{2,1,0:T(8,128)S(1)}) custom-call(s32[1]{0:T(128)} %bitcast.first_ref, s32[128,8]{1,0:T(8,128)S(1)} %copy.37.pairs_ref, s32[128]{0:T(128)S(1)} %copy-done.2, bf16[8,2,128,256]{3,2,1,0:T(8,128)(2,1)S(1)} %all-to-all-done.1.refs_0_, bf16[4608,256]{1,0:T(8,128)(2,1)S(1)} %copy-done.4, ...), custom_call_target="tpu_custom_call" | custom-call | flops 8000000000 | bytes 6000000 | tf_op jit(solution)/shard_map/audio_parts/pallas_call | solution.py:406
  67.4 1.0 copy-done.16
  68.4 9.6 %audio_parts.3 = (f32[14,256,128]{2,1,0:T(8,128)S(1)}, f32[14,8,256]{2,1,0:T(8,128)S(1)}) custom-call(s32[1]{0:T(128)} %bitcast.first_ref, s32[128,8]{1,0:T(8,128)S(1)} %copy.37.pairs_ref, s32[128]{0:T(128)S(1)} %copy-done.2, bf16[7,2,128,256]{3,2,1,0:T(8,128)(2,1)S(1)} %collective-permute-done.2.refs_0_, ...), custom_call_target="tpu_custom_call" | custom-call | flops 8000000000 | bytes 6000000 | tf_op jit(solution)/shard_map/audio_parts/pallas_call | solution.py:406
  78.0 0.5 collective-permute-start.5
  78.6 1.6 collective-permute-start.4
  80.2 5.8 %collective-permute-done.1.after_ref = bf16[7,2,128,256]{3,2,1,0:T(8,128)(2,1)S(1)} collective-permute-done((bf16[7,2,128,256]{3,2,1,0:T(8,128)(2,1)S(1)}, bf16[7,2,128,256]{3,2,1,0:T(8,128)(2,1)S(1)}, u32[]{:S(2)}, u32[]{:S(2)}) %collective-permute-start.1) | collective-permute-done | bytes 917536 | tf_op jit(solution)/shard_map/ppermute | solution.py:613
  86.0 43.7 %video_queries.1 = (bf16[4096,256]{1,0:T(8,128)(2,1)}, bf16[4096,256]{1,0:T(8,128)(2,1)}, bf16[7,2,128,256]{3,2,1,0:T(8,128)(2,1)S(1)}, f32[8,2,128,256]{3,2,1,0:T(8,128)S(1)}, bf16[7,2,128,256]{3,2,1,0:T(8,128)(2,1)S(1)}) custom-call(s32[1]{0:T(128)} %bitcast.first_ref, s32[128,8]{1,0:T(8,128)S(1)} %copy.29.pairs_ref, s32[128]{0:T(128)S(1)} %copy-done.11, ...), custom_call_target="tpu_custom_call" | custom-call | flops 20000000000 | bytes 20000000 | tf_op jit(solution)/shard_map/video_queries/pallas_call | solution.py:272
  129.7 1.9 collective-permute-start.8
  131.6 6.0 %collective-permute-start.9 = (bf16[7,2,128,256]{3,2,1,0:T(8,128)(2,1)S(1)}, bf16[7,2,128,256]{3,2,1,0:T(8,128)(2,1)S(1)}, u32[]{:S(2)}, u32[]{:S(2)}) collective-permute-start(bf16[7,2,128,256]{3,2,1,0:T(8,128)(2,1)S(1)} %get-tuple-element.49), channel_id=1, source_target_pairs={{0,8},{8,16},{16,24},{24,32},{32,40},{40,48},{48,56},{56,64},{64,7... | collective-permute-start | bytes 2752520 | tf_op jit(solution)/shard_map/ppermute | solution.py:618
  137.7 13.1 %audio_gradients.2 = (bf16[7,2,128,256]{3,2,1,0:T(8,128)(2,1)}, bf16[7,2,128,256]{3,2,1,0:T(8,128)(2,1)S(1)}, f32[4608,256]{1,0:T(8,128)S(1)}, f32[4608,256]{1,0:T(8,128)S(1)}) custom-call(s32[1]{0:T(128)} %bitcast.first_ref, s32[128,8]{1,0:T(8,128)S(1)} %copy.37.pairs_ref, s32[128]{0:T(128)S(1)} %copy-done.2, ...), custom_call_target="tpu_custom_call" | custom-call | flops 10000000000 | bytes 20000000 | tf_op jit(solution)/shard_map/audio_gradients/pallas_call | solution.py:574
  150.8 2.1 copy-done.12
  152.9 2.2 copy-done.14
  155.1 1.9 collective-permute-start.6
  157.0 6.0 %collective-permute-start.7 = (bf16[7,2,128,256]{3,2,1,0:T(8,128)(2,1)S(1)}, bf16[7,2,128,256]{3,2,1,0:T(8,128)(2,1)}, u32[]{:S(2)}, u32[]{:S(2)}) collective-permute-start(bf16[7,2,128,256]{3,2,1,0:T(8,128)(2,1)S(1)} %get-tuple-element.43), channel_id=1, source_target_pairs={{0,8},{8,16},{16,24},{24,32},{32,40},{40,48},{48,56},{56,64},{64,7... | collective-permute-start | bytes 2752520 | tf_op jit(solution)/shard_map/ppermute | solution.py:618
  163.1 1.4 add_convert_fusion
  164.5 4.7 %all-to-all-start.3 = ((bf16[8,2,128,256]{3,2,1,0:T(8,128)(2,1)}), bf16[8,2,128,256]{3,2,1,0:T(8,128)(2,1)}, u32[]{:S(2)}, u32[]{:S(2)}) async-start(bf16[8,2,128,256]{3,2,1,0:T(8,128)(2,1)} %add_convert_fusion), calls=%async_computation.3 | async-start | bytes 2097152 | tf_op jit(solution)/shard_map/all_to_all | solution.py:607
  169.3 1.7 copy-done.5
  170.9 1.7 copy-done.8
  172.6 2.3 copy-done.13
  174.9 2.3 copy-done.15
  177.3 1.2 copy-done.17
  178.5 30.2 %audio_gradients.3 = (f32[8,2,128,256]{3,2,1,0:T(8,128)S(1)}, bf16[8,512,256]{2,1,0:T(8,128)(2,1)}, bf16[8,512,256]{2,1,0:T(8,128)(2,1)}) custom-call(s32[1]{0:T(128)} %bitcast.first_ref, s32[128,8]{1,0:T(8,128)S(1)} %copy.37.pairs_ref, s32[128]{0:T(128)S(1)} %copy-done.2, bf16[8,2,128,256]{3,2,1,0:T(8,128)(2,1)S(1)} %all-to-all-done.1.refs_0_, ...), custom_call_target="tpu_custom_call" | custom-call | flops 10000000000 | bytes 20000000 | tf_op jit(solution)/shard_map/audio_gradients/pallas_call | solution.py:574
  208.7 2.6 %add_convert_fusion.1 = bf16[8,2,128,256]{3,2,1,0:T(8,128)(2,1)} fusion(f32[8,2,128,256]{3,2,1,0:T(8,128)S(1)} %get-tuple-element.41, bf16[7,2,128,256]{3,2,1,0:T(8,128)(2,1)} %collective-permute-done.7, bf16[7,2,128,256]{3,2,1,0:T(8,128)(2,1)S(1)} %collective-permute-done.6), kind=kLoop, calls=%fused_computation.1 | loop fusion | flops 2621440 | bytes 4980736 | tf_op jit(solution)/shard_map/convert_element_type | solution.py:680
  211.3 4.8 %all-to-all-start.2 = ((bf16[8,2,128,256]{3,2,1,0:T(8,128)(2,1)}), bf16[8,2,128,256]{3,2,1,0:T(8,128)(2,1)S(1)}, u32[]{:S(2)}, u32[]{:S(2)}) async-start(bf16[8,2,128,256]{3,2,1,0:T(8,128)(2,1)} %add_convert_fusion.1), calls=%async_computation.2 | async-start | bytes 2097152 | tf_op jit(solution)/shard_map/all_to_all | solution.py:607
  216.1 1.3 slice_bitcast_fusion
  217.4 0.3 copy.40
  217.6 1.0 copy.44
  218.7 0.3 copy.41
  218.9 1.0 copy.45
  219.9 12.1 %all-to-all-done.2 = bf16[8,2,128,256]{3,2,1,0:T(8,128)(2,1)S(1)} async-done(((bf16[8,2,128,256]{3,2,1,0:T(8,128)(2,1)}), bf16[8,2,128,256]{3,2,1,0:T(8,128)(2,1)S(1)}, u32[]{:S(2)}, u32[]{:S(2)}) %all-to-all-start.2) | async-done | bytes 1048608 | tf_op jit(solution)/shard_map/all_to_all | solution.py:607
  232.1 0.1 slice_bitcast_fusion.2
  232.2 0.3 copy.38
  232.4 1.0 copy.42
  233.4 0.3 copy.39
  233.7 1.0 copy.43
  (45 shorter events, 0.1 us)
Async XLA Ops:
  0.6 1.6 copy-start.18
  2.8 5.5 %copy-start.19 = (bf16[128,2048]{1,0:T(8,128)(2,1)S(1)}, bf16[128,2048]{1,0:T(8,128)(2,1)}, u32[]{:S(2)}) copy-start(bf16[128,2048]{1,0:T(8,128)(2,1)} %param.17) | copy-start | bytes 1572868
  3.8 4.9 %copy-start.20 = (bf16[128,2048]{1,0:T(8,128)(2,1)S(1)}, bf16[128,2048]{1,0:T(8,128)(2,1)}, u32[]{:S(2)}) copy-start(bf16[128,2048]{1,0:T(8,128)(2,1)} %param.18) | copy-start | bytes 1572868
  3.8 20.4 %all-to-all-start.1 = ((bf16[8,2,128,256]{3,2,1,0:T(8,128)(2,1)}), bf16[8,2,128,256]{3,2,1,0:T(8,128)(2,1)S(1)}, u32[]{:S(2)}, u32[]{:S(2)}) async-start(bf16[8,2,128,256]{3,2,1,0:T(8,128)(2,1)} %maximum_bitcast_fusion.1), calls=%async_computation.1 | async-start | bytes 2097152 | tf_op jit(solution)/shard_map/all_to_all | solution.py:603
  9.3 18.5 %copy-start.21 = (s32[128,8]{0,1:T(8,128)S(1)}, s32[128,8]{0,1:T(8,128)}, u32[]{:S(2)}) copy-start(s32[128,8]{0,1:T(8,128)} %param.21) | copy-start | bytes 12292
  9.3 18.6 %copy-start.22 = (s32[128,8]{0,1:T(8,128)S(1)}, s32[128,8]{0,1:T(8,128)}, u32[]{:S(2)}) copy-start(s32[128,8]{0,1:T(8,128)} %param.20) | copy-start | bytes 12292
  9.3 18.7 %copy-start.2 = (s32[128]{0:T(128)S(1)}, s32[128]{0:T(128)}, u32[]{:S(2)}) copy-start(s32[128]{0:T(128)} %len_ref.11) | copy-start | bytes 1540
  24.2 19.5 %all-to-all-start = ((bf16[8,2,128,256]{3,2,1,0:T(8,128)(2,1)}), bf16[8,2,128,256]{3,2,1,0:T(8,128)(2,1)S(1)}, u32[]{:S(2)}, u32[]{:S(2)}) async-start(bf16[8,2,128,256]{3,2,1,0:T(8,128)(2,1)} %maximum_bitcast_fusion), calls=%async_computation | async-start | bytes 2097152 | tf_op jit(solution)/shard_map/all_to_all | solution.py:603
  28.0 1.6 copy-start
  29.6 1.6 copy-start.1
  32.3 1.4 copy-start.3
  33.7 5.2 %copy-start.6 = (bf16[4608,256]{1,0:T(8,128)(2,1)}, bf16[4608,256]{1,0:T(8,128)(2,1)S(1)}, u32[]{:S(2)}) copy-start(bf16[4608,256]{1,0:T(8,128)(2,1)S(1)} %get-tuple-element.34.refs_2_.refs_3_.refs_7_.refs_6_) | copy-start | bytes 7077892
  35.4 32.9 %collective-permute-start.2 = (bf16[7,2,128,256]{3,2,1,0:T(8,128)(2,1)}, bf16[7,2,128,256]{3,2,1,0:T(8,128)(2,1)S(1)}, u32[]{:S(2)}, u32[]{:S(2)}) collective-permute-start(bf16[7,2,128,256]{3,2,1,0:T(8,128)(2,1)} %get-tuple-element.63), channel_id=1, source_target_pairs={{0,8},{8,16},{16,24},{24,32},{32,40},{40,48},{48,56},{56,64},{64,7... | collective-permute-start | bytes 2752520 | tf_op jit(solution)/shard_map/ppermute | solution.py:613
  39.0 29.4 %collective-permute-start.3 = (bf16[7,2,128,256]{3,2,1,0:T(8,128)(2,1)}, bf16[7,2,128,256]{3,2,1,0:T(8,128)(2,1)}, u32[]{:S(2)}, u32[]{:S(2)}) collective-permute-start(bf16[7,2,128,256]{3,2,1,0:T(8,128)(2,1)} %get-tuple-element.62), channel_id=1, source_target_pairs={{8,0},{16,8},{24,16},{32,24},{40,32},{48,40},{56,48},{64,56},{72,6... | collective-permute-start | bytes 2752520 | tf_op jit(solution)/shard_map/ppermute | solution.py:613
  43.7 6.3 %copy-start.4 = (bf16[4608,256]{1,0:T(8,128)(2,1)S(1)}, bf16[4608,256]{1,0:T(8,128)(2,1)}, u32[]{:S(2)}) copy-start(bf16[4608,256]{1,0:T(8,128)(2,1)} %copy-done.3) | copy-start | bytes 7077892
  43.8 36.4 %collective-permute-start = (bf16[7,2,128,256]{3,2,1,0:T(8,128)(2,1)S(1)}, bf16[7,2,128,256]{3,2,1,0:T(8,128)(2,1)S(1)}, u32[]{:S(2)}, u32[]{:S(2)}) collective-permute-start(bf16[7,2,128,256]{3,2,1,0:T(8,128)(2,1)S(1)} %get-tuple-element.65), channel_id=1, source_target_pairs={{0,8},{8,16},{16,24},{24,32},{32,40},{40,48},{48,56},{56,64},{64,7... | collective-permute-start | bytes 2752520 | tf_op jit(solution)/shard_map/ppermute | solution.py:613
  47.4 38.6 %collective-permute-start.1 = (bf16[7,2,128,256]{3,2,1,0:T(8,128)(2,1)S(1)}, bf16[7,2,128,256]{3,2,1,0:T(8,128)(2,1)S(1)}, u32[]{:S(2)}, u32[]{:S(2)}) collective-permute-start(bf16[7,2,128,256]{3,2,1,0:T(8,128)(2,1)S(1)} %get-tuple-element.64), channel_id=1, source_target_pairs={{8,0},{16,8},{24,16},{32,24},{40,32},{48,40},{56,48},{64,56},{72,6... | collective-permute-start | bytes 2752520 | tf_op jit(solution)/shard_map/ppermute | solution.py:613
  50.0 1.7 copy-start.7
  67.4 1.0 copy-start.16
  68.4 17.7 %copy-start.9 = (bf16[4096,256]{1,0:T(8,128)(2,1)S(1)}, bf16[4096,256]{1,0:T(8,128)(2,1)}, u32[]{:S(2)}) copy-start(bf16[4096,256]{1,0:T(8,128)(2,1)} %q_ref.1) | copy-start | bytes 6291460
  68.4 17.7 %copy-start.10 = (bf16[4096,256]{1,0:T(8,128)(2,1)S(1)}, bf16[4096,256]{1,0:T(8,128)(2,1)}, u32[]{:S(2)}) copy-start(bf16[4096,256]{1,0:T(8,128)(2,1)} %do_ref.1) | copy-start | bytes 6291460
  68.4 17.7 %copy-start.11 = (s32[128]{0:T(128)S(1)}, s32[128]{0:T(128)}, u32[]{:S(2)}) copy-start(s32[128]{0:T(128)} %len_ref.6) | copy-start | bytes 1540
  78.0 59.6 %collective-permute-start.5 = (f32[14,8,256]{2,1,0:T(8,128)S(1)}, f32[14,8,256]{2,1,0:T(8,128)S(1)}, u32[]{:S(2)}, u32[]{:S(2)}) collective-permute-start(f32[14,8,256]{2,1,0:T(8,128)S(1)} %pad_maximum_fusion.1), channel_id=1, source_target_pairs={{0,8},{8,16},{16,24},{24,32},{32,40},{40,48},{48,56},{56,64},{64,7... | collective-permute-start | bytes 344072 | tf_op jit(solution)/shard_map/ppermute | solution.py:662
  78.6 59.1 %collective-permute-start.4 = (f32[14,8,256]{2,1,0:T(8,128)S(1)}, f32[14,8,256]{2,1,0:T(8,128)S(1)}, u32[]{:S(2)}, u32[]{:S(2)}) collective-permute-start(f32[14,8,256]{2,1,0:T(8,128)S(1)} %pad_maximum_fusion), channel_id=1, source_target_pairs={{8,0},{16,8},{24,16},{32,24},{40,32},{48,40},{56,48},{64,56},{72,6... | collective-permute-start | bytes 344072 | tf_op jit(solution)/shard_map/ppermute | solution.py:661
  129.7 33.4 %collective-permute-start.8 = (bf16[7,2,128,256]{3,2,1,0:T(8,128)(2,1)S(1)}, bf16[7,2,128,256]{3,2,1,0:T(8,128)(2,1)S(1)}, u32[]{:S(2)}, u32[]{:S(2)}) collective-permute-start(bf16[7,2,128,256]{3,2,1,0:T(8,128)(2,1)S(1)} %get-tuple-element.48), channel_id=1, source_target_pairs={{8,0},{16,8},{24,16},{32,24},{40,32},{48,40},{56,48},{64,56},{72,6... | collective-permute-start | bytes 2752520 | tf_op jit(solution)/shard_map/ppermute | solution.py:618
  131.6 31.5 %collective-permute-start.9 = (bf16[7,2,128,256]{3,2,1,0:T(8,128)(2,1)S(1)}, bf16[7,2,128,256]{3,2,1,0:T(8,128)(2,1)S(1)}, u32[]{:S(2)}, u32[]{:S(2)}) collective-permute-start(bf16[7,2,128,256]{3,2,1,0:T(8,128)(2,1)S(1)} %get-tuple-element.49), channel_id=1, source_target_pairs={{0,8},{8,16},{16,24},{24,32},{32,40},{40,48},{48,56},{56,64},{64,7... | collective-permute-start | bytes 2752520 | tf_op jit(solution)/shard_map/ppermute | solution.py:618
  150.8 2.1 copy-start.12
  152.9 2.2 copy-start.14
  155.1 53.6 %collective-permute-start.6 = (bf16[7,2,128,256]{3,2,1,0:T(8,128)(2,1)}, bf16[7,2,128,256]{3,2,1,0:T(8,128)(2,1)S(1)}, u32[]{:S(2)}, u32[]{:S(2)}) collective-permute-start(bf16[7,2,128,256]{3,2,1,0:T(8,128)(2,1)} %get-tuple-element.42), channel_id=1, source_target_pairs={{8,0},{16,8},{24,16},{32,24},{40,32},{48,40},{56,48},{64,56},{72,6... | collective-permute-start | bytes 2752520 | tf_op jit(solution)/shard_map/ppermute | solution.py:618
  157.0 51.6 %collective-permute-start.7 = (bf16[7,2,128,256]{3,2,1,0:T(8,128)(2,1)S(1)}, bf16[7,2,128,256]{3,2,1,0:T(8,128)(2,1)}, u32[]{:S(2)}, u32[]{:S(2)}) collective-permute-start(bf16[7,2,128,256]{3,2,1,0:T(8,128)(2,1)S(1)} %get-tuple-element.43), channel_id=1, source_target_pairs={{0,8},{8,16},{16,24},{24,32},{32,40},{40,48},{48,56},{56,64},{64,7... | collective-permute-start | bytes 2752520 | tf_op jit(solution)/shard_map/ppermute | solution.py:618
  164.5 46.7 %all-to-all-start.3 = ((bf16[8,2,128,256]{3,2,1,0:T(8,128)(2,1)}), bf16[8,2,128,256]{3,2,1,0:T(8,128)(2,1)}, u32[]{:S(2)}, u32[]{:S(2)}) async-start(bf16[8,2,128,256]{3,2,1,0:T(8,128)(2,1)} %add_convert_fusion), calls=%async_computation.3 | async-start | bytes 2097152 | tf_op jit(solution)/shard_map/all_to_all | solution.py:607
  169.2 1.7 copy-start.5
  170.9 1.7 copy-start.8
  172.6 2.3 copy-start.13
  174.9 2.3 copy-start.15
  177.3 1.2 copy-start.17
  211.3 20.8 %all-to-all-start.2 = ((bf16[8,2,128,256]{3,2,1,0:T(8,128)(2,1)}), bf16[8,2,128,256]{3,2,1,0:T(8,128)(2,1)S(1)}, u32[]{:S(2)}, u32[]{:S(2)}) async-start(bf16[8,2,128,256]{3,2,1,0:T(8,128)(2,1)} %add_convert_fusion.1), calls=%async_computation.2 | async-start | bytes 2097152 | tf_op jit(solution)/shard_map/all_to_all | solution.py:607
